TPU v7x, 256 devices: a whole 4x4x8 slice. The times are simulated.
256 devices in a mesh: pipe: 16 (over x_lo, y, core), ctx: 16 (over z, x_hi).
Axes of the slice: x: 4 (x_hi: 2, x_lo: 2; x = x_hi * 2 + x_lo), y: 4, z: 8, core: 2. Of those that a mesh axis runs over, the one named last changes fastest.
Arguments:
- queries: bfloat16 [16, 2048, 4096], P('pipe', 'ctx'), may hold values from -6 to 6
- key_heads: bfloat16 [16, 2048, 512], P('pipe', 'ctx'), may hold values from -6 to 6
- value_heads: bfloat16 [16, 2048, 512], P('pipe', 'ctx'), may hold values from -0.59765625 to 0.59765625
- out_grad: bfloat16 [16, 2048, 4096], P('pipe', 'ctx'), may hold values from -6 to 6
- log_sum: bfloat16 [16, 32, 2048], P('pipe', None, 'ctx'), may hold values from 2 to 4
- row_delta: bfloat16 [16, 32, 2048], P('pipe', None, 'ctx'), may hold values from -5 to 5
- chosen: int32 [16, 4, 2], P('pipe'), may hold values from 0 to 2, as said below
Outputs:
- query_grads: bfloat16 [16, 2048, 4096], P('pipe', 'ctx')
- key_grads: bfloat16 [16, 2048, 512], P('pipe', 'ctx')
- value_grads: bfloat16 [16, 2048, 512], P('pipe', 'ctx')
- handed_back: bfloat16 [16, 2048, 4096], P('pipe', 'ctx')
Inputs may be any that keep to these rules, and one draw needn't show every extreme that they name: Row b of chosen[s] lists distinct key blocks below b first; a row with fewer than 2 earlier blocks is filled with b itself after them; the last row names block 2.
All inputs are finite; a program needn't handle non-finite values.
Results may differ from a plain program's by a relative error of at most 0.0052.
Values may be sent and summed in bfloat16 or wider, within the bound.
A program may use at most 128 MiB of HBM per device.

v0:
```python
import jax
import jax.numpy as jnp
from jax import lax
from jax.sharding import PartitionSpec as P

H = 32
KVH = 4
HD = 128
BLOCK = 512
SEL = 2


def passed_along(block, axis, distance):
    devices = range(lax.axis_size(axis))
    route = [(i - distance, i) for i in devices if i - distance in devices]
    return lax.ppermute(block, axis, route)


def add_rows(buffer, part, first_row):
    current = lax.dynamic_slice_in_dim(buffer, first_row, part.shape[0], 0)
    return lax.dynamic_update_slice_in_dim(buffer, current + part, first_row, 0)


def per_device(queries, key_heads, value_heads, out_grad, log_sum, row_delta, chosen):
    position = lax.axis_index("ctx")
    tokens_here = queries.shape[1]
    all_keys, all_values = (
        lax.all_gather(key_heads[0], "ctx", axis=0, tiled=True),
        lax.all_gather(value_heads[0], "ctx", axis=0, tiled=True),
    )
    seq_total = all_keys.shape[0]
    kv_width = all_keys.shape[1]
    block_lists = chosen[0]
    groups = H // KVH
    softmax_scale = HD ** (-0.5)
    zero_buffer = jnp.zeros((seq_total, kv_width), jnp.float32)
    query_rows = queries[0]
    first_row = position * tokens_here
    buffers = (zero_buffer, zero_buffer)
    row_count = query_rows.shape[0]
    home_block = first_row // BLOCK
    query_per_head = query_rows.reshape(row_count, KVH, groups, HD)
    gradient_per_head = out_grad[0].reshape(row_count, KVH, groups, HD)
    row_sums = log_sum[0].astype(jnp.float32).reshape(KVH, groups, row_count)
    deltas = row_delta[0].astype(jnp.float32).reshape(KVH, groups, row_count)
    row_place = first_row + jnp.arange(row_count, dtype=jnp.int32)

    def apply(key_first, allowed, carried):
        query_gradient_total, key_acc, value_acc = carried
        key_tile = lax.dynamic_slice_in_dim(all_keys, key_first, BLOCK, 0).reshape(BLOCK, KVH, HD)
        value_tile = lax.dynamic_slice_in_dim(all_values, key_first, BLOCK, 0).reshape(
            BLOCK, KVH, HD
        )
        attention_logits = (
            jnp.einsum(
                "oifl,mil->ifom", query_per_head, key_tile, preferred_element_type=jnp.float32
            )
            * softmax_scale
        )
        attn_probs = jnp.where(allowed, jnp.exp(attention_logits - row_sums[..., None]), 0.0)
        probability_reduced = attn_probs.astype(jnp.bfloat16)
        value_portion = jnp.einsum(
            "imho,himp->oip",
            probability_reduced,
            gradient_per_head,
            preferred_element_type=jnp.float32,
        )
        probability_gradient = jnp.einsum(
            "oifl,mil->ifom", gradient_per_head, value_tile, preferred_element_type=jnp.float32
        )
        logit_gradient = (attn_probs * (probability_gradient - deltas[..., None])).astype(
            jnp.bfloat16
        )
        query_gradient_total = (
            query_gradient_total
            + jnp.einsum(
                "mtuf,fmw->umtw", logit_gradient, key_tile, preferred_element_type=jnp.float32
            )
            * softmax_scale
        )
        key_portion = (
            jnp.einsum(
                "imho,himp->oip", logit_gradient, query_per_head, preferred_element_type=jnp.float32
            )
            * softmax_scale
        )
        key_acc = add_rows(key_acc, key_portion.reshape(BLOCK, kv_width), key_first)
        value_acc = add_rows(value_acc, value_portion.reshape(BLOCK, kv_width), key_first)
        return (query_gradient_total, key_acc, value_acc)

    carried = (jnp.zeros((row_count, KVH, groups, HD), jnp.float32), buffers[0], buffers[1])
    for entry_index in range(SEL):
        target = block_lists[home_block, entry_index]
        carried = lax.cond(
            target < home_block,
            lambda carry_in, target=target: apply(target * BLOCK, True, carry_in),
            lambda carry_in: carry_in,
            carried,
        )
    own_first = home_block * BLOCK
    causal = (own_first + jnp.arange(BLOCK, dtype=jnp.int32))[None, :] <= row_place[:, None]
    carried = apply(own_first, causal, carried)
    row_grad_out = carried[0].reshape(row_count, H * HD)
    buffers = (carried[1], carried[2])
    query_grads = row_grad_out.astype(jnp.bfloat16)
    key_buffer, value_buffer = buffers
    key_grads, value_grads = (
        lax.psum_scatter(key_buffer, "ctx", scatter_dimension=0, tiled=True),
        lax.psum_scatter(value_buffer, "ctx", scatter_dimension=0, tiled=True),
    )
    query_grads = query_grads[None]
    handed_back = passed_along(query_grads, "pipe", -1)
    return (
        query_grads,
        key_grads[None].astype(jnp.bfloat16),
        value_grads[None].astype(jnp.bfloat16),
        handed_back,
    )


def solution(mesh):
    return jax.shard_map(
        per_device,
        mesh=mesh,
        in_specs=(
            P("pipe", "ctx", None),
            P("pipe", "ctx", None),
            P("pipe", "ctx", None),
            P("pipe", "ctx", None),
            P("pipe", None, "ctx"),
            P("pipe", None, "ctx"),
            P("pipe", None, None),
        ),
        out_specs=(
            P("pipe", "ctx", None),
            P("pipe", "ctx", None),
            P("pipe", "ctx", None),
            P("pipe", "ctx", None),
        ),
        check_vma=False,
    )
```

profile of v0, /device:TPU:8, one launch (start us, length us, event | category | flops | bytes accessed | tf_op | source)
XLA Modules:
  0.0 678.3 jit_solution(11776297619159675587)
XLA Ops:
  7.2 1.7 copy.53
  9.0 1.7 copy.55
  16.1 82.8 %all-gather.5.cloned.1.call-done = bf16[1,2048,512]{1,2,0:T(8,128)(2,1)} async-done(((bf16[1,128,512]{1,2,0:T(8,128)(2,1)}), bf16[1,2048,512]{1,2,0:T(8,128)(2,1)}) %all-gather.5.cloned.1.call-update) | async-done | bytes 2097168 | tf_op jit(solution)/shard_map/all_gather | solution.py:28
  100.0 4.5 fusion.34
  104.5 79.1 %all-gather.7.cloned.1.call-done = bf16[1,2048,512]{1,2,0:T(8,128)(2,1)} async-done(((bf16[1,128,512]{1,2,0:T(8,128)(2,1)}), bf16[1,2048,512]{1,2,0:T(8,128)(2,1)}) %all-gather.7.cloned.1.call-update) | async-done | bytes 2097168 | tf_op jit(solution)/shard_map/all_gather | solution.py:29
  184.7 5.0 fusion.21
  189.7 2.5 fusion.29
  192.2 2.5 copy.64
  194.7 6.5 conditional.2
  194.7 2.5 broadcast_in_dim.16
  197.2 2.5 broadcast_in_dim.16.clone
  201.2 10.7 %conditional.3 = (f32[128,4,8,128]{0,3,2,1:T(8,128)}, f32[2048,512]{1,0:T(8,128)}, f32[2048,512]{1,0:T(8,128)}) conditional(s32[]{:T(128)} %convert_element_type.79, (f32[128,4,8,128]{0,3,2,1:T(8,128)}, f32[2048,512]{0,1:T(8,128)}, f32[2048,512]{0,1:T(8,128)}) %conditional.2, (s32[]{:T(128)}, bf16[2048,512]{0,1:T(8,128)(2,1)}, ...), branch_computations={%region_2.3_spmd, %region_3.4_spmd} | conditional | flops 2702966784 | bytes 91799656 | solution.py:94
  201.2 5.4 copy.114
  206.6 5.4 copy.116
  211.9 2.8 add_dynamic-update-slice_fusion.1
  214.8 5.1 fusion.25
  220.3 2.5 add_dynamic-update-slice_fusion
  222.8 3.8 fusion.28
  227.1 1.9 collective-permute-start
  229.0 12.3 %collective-permute-done = bf16[1,128,4096]{2,1,0:T(8,128)(2,1)S(1)} collective-permute-done((bf16[1,128,4096]{2,1,0:T(8,128)(2,1)S(1)}, bf16[1,128,4096]{2,1,0:T(8,128)(2,1)S(1)}, u32[]{:S(2)}, u32[]{:S(2)}) %collective-permute-start) | collective-permute-done | bytes 1048608 | tf_op jit(solution)/shard_map/ppermute | solution.py:16
  241.3 213.1 %reduce-scatter.3.cloned.1.call-done = f32[128,512]{1,0:T(8,128)} async-done(((f32[2048,512]{1,0:T(8,128)}), f32[128,512]{1,0:T(8,128)}) %reduce-scatter.3.cloned.1.call-update) | async-done | bytes 262160 | tf_op jit(solution)/shard_map/reduce_scatter | solution.py:108
  454.5 1.6 convert_bitcast_fusion.1
  456.1 213.1 %reduce-scatter.5.cloned.1.call-done = f32[128,512]{1,0:T(8,128)} async-done(((f32[2048,512]{1,0:T(8,128)}), f32[128,512]{1,0:T(8,128)}) %reduce-scatter.5.cloned.1.call-update) | async-done | bytes 262160 | tf_op jit(solution)/shard_map/reduce_scatter | solution.py:109
  669.1 1.6 convert_bitcast_fusion
  (31 shorter events, 9.8 us)
Async XLA Ops:
  7.2 6.8 %copy-start.5 = (s32[1,4,2]{1,2,0:T(2,128)S(1)}, s32[1,4,2]{1,2,0:T(2,128)}, u32[]{:S(2)}) copy-start(s32[1,4,2]{1,2,0:T(2,128)} %param.17) | copy-start | bytes 100
  7.2 8.7 %copy-start.4 = (bf16[1,32,128]{2,1,0:T(8,128)(2,1)S(1)}, bf16[1,32,128]{2,1,0:T(8,128)(2,1)}, u32[]{:S(2)}) copy-start(bf16[1,32,128]{2,1,0:T(8,128)(2,1)} %param.15) | copy-start | bytes 24580
  7.2 8.7 %copy-start.3 = (bf16[1,32,128]{2,1,0:T(8,128)(2,1)S(1)}, bf16[1,32,128]{2,1,0:T(8,128)(2,1)}, u32[]{:S(2)}) copy-start(bf16[1,32,128]{2,1,0:T(8,128)(2,1)} %param.16) | copy-start | bytes 24580
  7.2 91.7 %all-gather.5.cloned.1.call-start = ((), (), s32[]{:S(2)}) async-start(), calls=%async_computation.4 | async-start | bytes 2228224 | tf_op jit(solution)/shard_map/all_gather | solution.py:28
  8.9 174.7 %all-gather.7.cloned.1.call-start = ((), (), s32[]{:S(2)}) async-start(), calls=%async_computation.5 | async-start | bytes 2228224 | tf_op jit(solution)/shard_map/all_gather | solution.py:29
  10.7 443.8 %reduce-scatter.3.cloned.1.call-start = ((), (), s32[]{:S(2)}) async-start(), calls=%async_computation.2 | async-start | bytes 4456448 | tf_op jit(solution)/shard_map/reduce_scatter | solution.py:108
  189.7 2.5 copy-start.1
  214.8 454.4 %reduce-scatter.5.cloned.1.call-start = ((), (), s32[]{:S(2)}) async-start(), calls=%async_computation.3 | async-start | bytes 4456448 | tf_op jit(solution)/shard_map/reduce_scatter | solution.py:109
  227.1 444.7 %copy-start.2 = (bf16[1,128,4096]{2,1,0:T(8,128)(2,1)}, bf16[1,128,4096]{2,1,0:T(8,128)(2,1)S(1)}, u32[]{:S(2)}) copy-start(bf16[1,128,4096]{2,1,0:T(8,128)(2,1)S(1)} %copy.71) | copy-start | bytes 3145732
  227.1 14.2 %collective-permute-start = (bf16[1,128,4096]{2,1,0:T(8,128)(2,1)S(1)}, bf16[1,128,4096]{2,1,0:T(8,128)(2,1)S(1)}, u32[]{:S(2)}, u32[]{:S(2)}) collective-permute-start(bf16[1,128,4096]{2,1,0:T(8,128)(2,1)S(1)} %copy.71), channel_id=1, source_target_pairs={{16,0},{32,16},{48,32},{64,48},{80,64},{96,80},{112,96},{128,112},... | collective-permute-start | bytes 3145736 | tf_op jit(solution)/shard_map/ppermute | solution.py:16
Sparse Core Ops, SparseCore 0:
  11.1 87.7 all-gather.4
  101.9 81.6 all-gather.6
  214.9 239.5 reduce-scatter.2
  458.9 210.2 reduce-scatter.4
where the time goes:
time: 679 us; the launch traced here: 678 us
  waiting for transfers between devices  600 us (88%)
  local copies, waits for them, and re-layouts  31 us (5%)
  matrix products  20.9 us (3%)
  between operations  15.2 us (2%)
  other arithmetic  8.67 us (1%)
    reduce_scatter x1, waiting for transfers between devices, per_device(): lax.psum_scatter(key_buffer, 'ctx', scatter_dimension=0, tiled=True)  213 us
    reduce_scatter x1, waiting for transfers between devices, per_device(): lax.psum_scatter(value_buffer, 'ctx', scatter_dimension=0, tiled=True)  213 us
    all_gather x1, waiting for transfers between devices, per_device(): lax.all_gather(key_heads[0], 'ctx', axis=0, tiled=True)  82.8 us
    all_gather x1, waiting for transfers between devices, per_device(): lax.all_gather(value_heads[0], 'ctx', axis=0, tiled=True)  79.1 us
  transfers between devices with their start and end apart: 5, of which 5 were waited for; matrix products, arithmetic and copies ran while one was open for 4% of the time, Pallas kernels for 0%

commit v1 on v0

v1 whole, which is shorter than its diff:
```python
import jax
import jax.numpy as jnp
from jax import lax
from jax.experimental import pallas as pl
from jax.experimental.pallas import tpu as pltpu
from jax.sharding import PartitionSpec as P

H = 32
KVH = 4
HD = 128
BLOCK = 512
ROWS = 128
PAIR = 2 * ROWS
SLOTS = 6
LEVELS = 8
LOG2E = 1.4426950408889634
SCALE = HD**-0.5
HEADS = 4
NT = (((1,), (1,)), ((), ()))
NN = (((1,), (0,)), ((), ()))
TN = (((0,), (0,)), ((), ()))
MESH = pl.DeviceIdType.MESH
F32 = jnp.float32
BF16 = jnp.bfloat16


def kernel(
    chosen_ref, q_ref, k_ref, v_ref, g_ref, lse_ref, delta_ref,
    dq_ref, dk_ref, dv_ref, hb_ref,
    qa, ga, kv, wr, acc, dqt, stat, stat_in, rs, rr, es, er, dq_out, fin,
    own_sem, x_s, x_r, qx_s, qx_r, up_s, up_r, w_s, w_r, e_s, e_r,
    rd_s, rd_r, er_s, er_r, dq_s, dq_r, hb_s, hb_r, f_s, f_r,
):
    pipe = lax.axis_index("pipe")
    place = lax.axis_index("ctx")
    z = place // 2
    xh = place % 2
    xo = 1 - xh
    partner = (pipe, z * 2 + xo)
    above = (pipe, ((z + 1) % LEVELS) * 2 + xh)
    below = (pipe, ((z + LEVELS - 1) % LEVELS) * 2 + xh)
    before = ((pipe + 15) % 16, place)
    after = ((pipe + 1) % 16, place)
    chain = jnp.where(z <= 5, z, z - 4)
    chain_above = jnp.where(z <= 4, z + 1, jnp.where(z == 7, 0, z - 3))
    wrap = jnp.where(z == 7, 4, jnp.where(z <= 2, 3 - z, 0))
    wrap_below = jnp.where(z <= 3, 4 - z, 0)
    last_block = z >= 6
    second = (chosen_ref[0, 3, 0] + chosen_ref[0, 3, 1]) == 3

    def remote(src, dst, send, recv, device):
        return pltpu.make_async_remote_copy(
            src_ref=src, dst_ref=dst, send_sem=send, recv_sem=recv,
            device_id=device, device_id_type=MESH,
        )

    def lanes(start, size):
        return pl.ds(pl.multiple_of(start, 128), size)

    def rows(start, size):
        return pl.ds(pl.multiple_of(start, 128), size)

    def kv_swap(j, t):
        src = (k_ref, v_ref)[t]
        return remote(
            src.at[0, :, lanes((2 * xo + j) * HD, HD)],
            kv.at[j, 0, t, rows(xh * ROWS, ROWS)],
            x_s.at[j, t], x_r.at[j, t], partner,
        )

    def kv_own(j, t):
        src = (k_ref, v_ref)[t]
        return pltpu.make_async_copy(
            src.at[0, :, lanes((2 * xh + j) * HD, HD)],
            kv.at[j, 0, t, rows(xh * ROWS, ROWS)],
            own_sem.at[j, t],
        )

    def q_swap(j, t):
        src, dst = ((q_ref, qa), (g_ref, ga))[t]
        return remote(
            src.at[0, :, lanes(xo * 2048 + j * 1024, 1024)],
            dst.at[xh, :, pl.ds(j * 1024, 1024)],
            qx_s.at[j, t], qx_r.at[j, t], partner,
        )

    def q_own(j, t):
        src, dst = ((q_ref, qa), (g_ref, ga))[t]
        return pltpu.make_async_copy(
            src.at[0, :, lanes(xh * 2048 + j * 1024, 1024)],
            dst.at[xh, :, pl.ds(j * 1024, 1024)],
            own_sem.at[2 + j, t],
        )

    def stat_swap(t):
        src = (lse_ref, delta_ref)[t]
        return remote(
            src.at[0, pl.ds(pl.multiple_of(xo * 16, 16), 16)],
            stat_in.at[t], x_s.at[2, t], x_r.at[2, t], partner,
        )

    def up(j, d):
        return remote(kv.at[j, d], kv.at[j, d + 1], up_s.at[j, d], up_r.at[j, d + 1], above)

    def up_in(j, d):
        return remote(kv.at[j, d - 1], kv.at[j, d], up_s.at[j, d - 1], up_r.at[j, d], above)

    def round_first(j):
        return remote(kv.at[j, 0], wr.at[j, 0], w_s.at[j, 0], w_r.at[j, 0], below)

    def round_on(j, w):
        return remote(wr.at[j, w - 1], wr.at[j, w], w_s.at[j, w], w_r.at[j, w], below)

    def round_in(j, w):
        return remote(wr.at[j, w], wr.at[j, w], w_s.at[j, w], w_r.at[j, w], below)

    def extra(j, d):
        return remote(kv.at[j, d], kv.at[j, d], e_s.at[j, d - 4], e_r.at[j, d - 4], below)

    def down(j, d):
        return remote(rs.at[j, d], rr.at[j, d - 1], rd_s.at[j, d], rd_r.at[j, d - 1], below)

    def down_in(j, d):
        return remote(rs.at[j, d + 1], rr.at[j, d], rd_s.at[j, d + 1], rd_r.at[j, d], below)

    def extra_back(j, e):
        return remote(es.at[j, e], er.at[j, e], er_s.at[j, e], er_r.at[j, e], above)

    def extra_on(j, e):
        return remote(er.at[j, e], er.at[j, e], er_s.at[j, e], er_r.at[j, e], above)

    def dq_swap(j):
        return remote(
            dq_out.at[j], dq_ref.at[0, :, lanes(xh * 2048 + j * 1024, 1024)],
            dq_s.at[j], dq_r.at[j], partner,
        )

    def dq_in(j):
        return remote(
            dq_out.at[j], dq_ref.at[0, :, lanes(xo * 2048 + j * 1024, 1024)],
            dq_s.at[j], dq_r.at[j], partner,
        )

    def hand_back(j, column):
        part = lanes(column * 2048 + j * 1024, 1024)
        return remote(
            dq_ref.at[0, :, part], hb_ref.at[0, :, part],
            hb_s.at[j, column], hb_r.at[j, column], before,
        )

    def fin_swap(j, t):
        dst = (dk_ref, dv_ref)[t]
        return remote(
            fin.at[j, t, rows(xo * ROWS, ROWS)],
            dst.at[0, :, lanes((2 * xh + j) * HD, HD)],
            f_s.at[j, t], f_r.at[j, t], partner,
        )

    def unit(j, r, d, first, masked=False):
        keys = kv[j, d, 0]
        values = kv[j, d, 1]
        d_keys = None
        d_values = None
        for c in range(8 // HEADS):
            base = j * 1024 + c * HEADS * HD
            head = j * 8 + c * HEADS
            queries = jnp.concatenate(
                [qa[r, :, base + i * HD : base + (i + 1) * HD] for i in range(HEADS)], axis=0
            )
            grads = jnp.concatenate(
                [ga[r, :, base + i * HD : base + (i + 1) * HD] for i in range(HEADS)], axis=0
            )
            lse = jnp.concatenate(
                [stat[0, r, pl.ds(head + i, 1), :] for i in range(HEADS)], axis=1
            )
            delta = jnp.concatenate(
                [stat[1, r, pl.ds(head + i, 1), :] for i in range(HEADS)], axis=1
            )
            scores = lax.dot_general(keys, queries, NT, preferred_element_type=F32)
            probs = jnp.exp2(scores * (SCALE * LOG2E) - lse)
            if masked:
                shape = (PAIR, HEADS * HD)
                key_at = lax.broadcasted_iota(jnp.int32, shape, 0)
                query_at = lax.broadcasted_iota(jnp.int32, shape, 1) % HD + r * ROWS
                probs = jnp.where(key_at <= query_at, probs, 0.0)
            prob_grads = lax.dot_general(values, grads, NT, preferred_element_type=F32)
            score_grads = (probs * (prob_grads - delta)).astype(BF16)
            probs_low = probs.astype(BF16)
            part_v = lax.dot_general(probs_low, grads, NN, preferred_element_type=F32)
            part_k = lax.dot_general(score_grads, queries, NN, preferred_element_type=F32)
            d_values = part_v if d_values is None else d_values + part_v
            d_keys = part_k if d_keys is None else d_keys + part_k
            dqt[r, :, base : base + HEADS * HD] += lax.dot_general(
                keys, score_grads, TN, preferred_element_type=F32
            )
        if first:
            acc[j, d, 0] = d_keys
            acc[j, d, 1] = d_values
        else:
            acc[j, d, 0] += d_keys
            acc[j, d, 1] += d_values

    def has(d):
        return (d <= chain) | (last_block & (d >= 4))

    def gather_step(j, k):
        @pl.when(k <= chain)
        def _():
            up_in(j, k).wait_recv()

        @pl.when(k + 1 <= chain_above)
        def _():
            up(j, k).start()

        @pl.when(k <= wrap)
        def _():
            round_in(j, k - 1).wait_recv()

        @pl.when(k + 1 <= wrap_below)
        def _():
            round_on(j, k).start()

        @pl.when((z == 7) & ((k == 3) | (k == 4)))
        def _():
            kv[j, k + 1] = jnp.where(second, wr[j, k - 1], wr[j, k - 3])
            extra(j, k + 1).start()

        @pl.when((z == 6) & (k >= 4))
        def _():
            extra(j, k).wait_recv()

    def starts_chain(d):
        return d + 1 > chain_above

    def send_down(j, d, ready):
        @pl.when((d <= chain) & starts_chain(d) & ready)
        def _():
            rs[j, d] = acc[j, d].astype(BF16)
            down(j, d).start()

        @pl.when((d <= chain) & jnp.logical_not(starts_chain(d)) & jnp.logical_not(ready))
        def _():
            down_in(j, d).wait_recv()
            rs[j, d] = (acc[j, d] + rr[j, d].astype(F32)).astype(BF16)
            down(j, d).start()

        @pl.when((z == 6) & (d >= 4) & ready)
        def _():
            es[j, d - 4] = acc[j, d].astype(BF16)
            extra_back(j, d - 4).start()

        @pl.when((z == 7) & (d >= 4) & jnp.logical_not(ready))
        def _():
            extra_on(j, d - 4).wait_recv()
            es[j, d - 4] = (acc[j, d] + er[j, d - 4].astype(F32)).astype(BF16)
            extra_back(j, d - 4).start()

    def pass_extra(j, e):
        @pl.when((z <= 2) | ((z == 3) & (e == 1)))
        def _():
            extra_on(j, e).wait_recv()

        @pl.when((z <= 1) | ((z == 2) & (e == 1)))
        def _():
            extra_on(j, e).start()

    def finish_keys(j):
        @pl.when(z <= 6)
        def _():
            down_in(j, 0).wait_recv()
            acc[j, 0] += rr[j, 0].astype(F32)

        @pl.when(z <= 3)
        def _():
            mine = second == (z >= 2)
            acc[j, 0] += jnp.where(mine, er[j, z % 2].astype(F32), 0.0)

        fin[j, 0] = (acc[j, 0, 0] * SCALE).astype(BF16)
        fin[j, 1] = acc[j, 0, 1].astype(BF16)
        for t in range(2):
            fin_swap(j, t).start()
        columns = lanes((2 * xh + j) * HD, HD)
        dk_ref[0, :, columns] = fin[j, 0, rows(xh * ROWS, ROWS)]
        dv_ref[0, :, columns] = fin[j, 1, rows(xh * ROWS, ROWS)]

    def finish_queries(j):
        for i in range(8):
            cols = slice(j * 1024 + i * HD, j * 1024 + (i + 1) * HD)
            dq_out[j, :, i * HD : (i + 1) * HD] = (dqt[xo, :, cols].T * SCALE).astype(BF16)
        dq_swap(j).start()
        for i in range(8):
            cols = slice(j * 1024 + i * HD, j * 1024 + (i + 1) * HD)
            dq_ref[0, :, lanes(xh * 2048 + j * 1024 + i * HD, HD)] = (
                dqt[xh, :, cols].T * SCALE
            ).astype(BF16)

        @pl.when(pipe > 0)
        def _():
            hand_back(j, xh).start()

    def hand_on(j):
        dq_in(j).wait_recv()

        @pl.when(pipe > 0)
        def _():
            hand_back(j, xo).start()

    barrier = pltpu.get_barrier_semaphore()
    for device in (partner, above, below, before, after):
        pl.semaphore_signal(barrier, inc=1, device_id=device, device_id_type=MESH)
    pl.semaphore_wait(barrier, 5)

    for j in range(2):
        for t in range(2):
            kv_swap(j, t).start()
            kv_own(j, t).start()
    for t in range(2):
        stat_swap(t).start()
        for j in range(2):
            q_own(j, t).start()

    dqt[...] = jnp.zeros_like(dqt)
    own_rows = pl.ds(pl.multiple_of(xh * 16, 16), 16)
    stat[0, xh] = lse_ref[0, own_rows].astype(F32) * LOG2E
    stat[1, xh] = delta_ref[0, own_rows].astype(F32)

    @pl.when(pipe == 15)
    def _():
        hb_ref[...] = jnp.zeros_like(hb_ref)

    for j in range(2):
        for t in range(2):
            kv_own(j, t).wait()
            q_own(j, t).wait()

    def first_step(j):
        for t in range(2):
            kv_swap(j, t).wait_recv()

        @pl.when(chain_above >= 1)
        def _():
            up(j, 0).start()

        @pl.when(wrap_below >= 1)
        def _():
            round_first(j).start()

    first_step(0)
    for t in range(2):
        q_swap(0, t).start()
    for t in range(2):
        stat_swap(t).wait_recv()
    stat[0, xo] = stat_in[0].astype(F32) * LOG2E
    stat[1, xo] = stat_in[1].astype(F32)

    unit(0, xh, 0, True, True)

    def phase_a(k, carry):
        gather_step(0, k)

        @pl.when(has(k))
        def _():
            unit(0, xh, k, True)

        return carry

    lax.fori_loop(1, SLOTS, phase_a, 0)
    first_step(1)
    for t in range(2):
        q_swap(0, t).wait_recv()
        q_swap(1, t).start()

    unit(1, xh, 0, True, True)

    def phase_b(k, carry):
        gather_step(1, k)
        far = SLOTS - k

        @pl.when(has(far))
        def _():
            unit(0, xo, far, False)

        send_down(0, far, True)

        @pl.when(has(k))
        def _():
            unit(1, xh, k, True)

        return carry

    lax.fori_loop(1, SLOTS, phase_b, 0)
    unit(0, xo, 0, False, True)
    finish_queries(0)
    for t in range(2):
        q_swap(1, t).wait_recv()

    def phase_c(k, carry):
        far = SLOTS - k

        @pl.when(has(far))
        def _():
            unit(1, xo, far, False)

        send_down(1, far, True)
        send_down(0, far, False)
        return carry

    lax.fori_loop(1, SLOTS, phase_c, 0)
    unit(1, xo, 0, False, True)
    finish_queries(1)
    hand_on(0)
    for e in range(2):
        pass_extra(0, e)
    finish_keys(0)

    def phase_d(k, carry):
        send_down(1, SLOTS - k, False)
        return carry

    lax.fori_loop(1, SLOTS, phase_d, 0)
    hand_on(1)
    for e in range(2):
        pass_extra(1, e)
    finish_keys(1)

    for j in range(2):
        for t in range(2):
            fin_swap(j, t).wait_recv()
            fin_swap(j, t).wait_send()
            kv_swap(j, t).wait_send()
            q_swap(j, t).wait_send()
        dq_swap(j).wait_send()

        @pl.when(pipe > 0)
        def _():
            for column in range(2):
                hand_back(j, column).wait_send()

        @pl.when(pipe < 15)
        def _():
            for column in range(2):
                hand_back(j, column).wait_recv()

        for d in range(SLOTS):
            @pl.when(d + 1 <= chain_above)
            def _():
                up(j, d).wait_send()

            if d >= 1:
                @pl.when(d <= chain)
                def _():
                    down(j, d).wait_send()

            if d >= 4:
                @pl.when(z == 7)
                def _():
                    extra(j, d).wait_send()

        for w in range(4):
            @pl.when(w + 1 <= wrap_below)
            def _():
                round_on(j, max(w, 1)).wait_send() if w else round_first(j).wait_send()

        for e in range(2):
            @pl.when(last_block)
            def _():
                extra_back(j, e).wait_send()

            @pl.when((z <= 1) | ((z == 2) & (e == 1)))
            def _():
                extra_on(j, e).wait_send()
    for t in range(2):
        stat_swap(t).wait_send()


def per_device(queries, key_heads, value_heads, out_grad, log_sum, row_delta, chosen):
    vmem = pl.BlockSpec(memory_space=pltpu.VMEM)
    dma = pltpu.SemaphoreType.DMA
    level = (2, PAIR, HD)
    flops = 5 * 2 * ROWS * H * HD * 1536
    return pl.pallas_call(
        kernel,
        out_shape=(
            jax.ShapeDtypeStruct(queries.shape, BF16),
            jax.ShapeDtypeStruct(key_heads.shape, BF16),
            jax.ShapeDtypeStruct(value_heads.shape, BF16),
            jax.ShapeDtypeStruct(queries.shape, BF16),
        ),
        in_specs=[pl.BlockSpec(memory_space=pltpu.SMEM)] + [vmem] * 6,
        out_specs=(vmem,) * 4,
        scratch_shapes=[
            pltpu.VMEM((2, ROWS, 2048), BF16),
            pltpu.VMEM((2, ROWS, 2048), BF16),
            pltpu.VMEM((2, SLOTS) + level, BF16),
            pltpu.VMEM((2, 4) + level, BF16),
            pltpu.VMEM((2, SLOTS) + level, F32),
            pltpu.VMEM((2, HD, 2048), F32),
            pltpu.VMEM((2, 2, 16, ROWS), F32),
            pltpu.VMEM((2, 16, ROWS), BF16),
            pltpu.VMEM((2, SLOTS) + level, BF16),
            pltpu.VMEM((2, SLOTS) + level, BF16),
            pltpu.VMEM((2, 2) + level, BF16),
            pltpu.VMEM((2, 2) + level, BF16),
            pltpu.VMEM((2, ROWS, 1024), BF16),
            pltpu.VMEM((2,) + level, BF16),
            dma((4, 2)),
            dma((3, 2)), dma((3, 2)),
            dma((2, 2)), dma((2, 2)),
            dma((2, SLOTS)), dma((2, SLOTS)),
            dma((2, 4)), dma((2, 4)),
            dma((2, 2)), dma((2, 2)),
            dma((2, SLOTS)), dma((2, SLOTS)),
            dma((2, 2)), dma((2, 2)),
            dma((2,)), dma((2,)),
            dma((2, 2)), dma((2, 2)),
            dma((2, 2)), dma((2, 2)),
        ],
        compiler_params=pltpu.CompilerParams(
            collective_id=0, has_side_effects=True, vmem_limit_bytes=40 * 2**20
        ),
        cost_estimate=pl.CostEstimate(
            flops=flops, bytes_accessed=6 * 2**20, transcendentals=ROWS * H * 1536
        ),
        name="block_attention_backward",
    )(chosen, queries, key_heads, value_heads, out_grad, log_sum, row_delta)


def solution(mesh):
    heads = P("pipe", "ctx", None)
    stats = P("pipe", None, "ctx")
    return jax.shard_map(
        per_device,
        mesh=mesh,
        in_specs=(heads, heads, heads, heads, stats, stats, P("pipe", None, None)),
        out_specs=(heads, heads, heads, heads),
        check_vma=False,
    )
```

time: 679 us -> 107 us (0.16)
  the two profiles are of different devices: /device:TPU:8 before, /device:TPU:100 now
where the time goes in v1:
time: 107 us
  Pallas kernels  96.5 us (90%)
  local copies, waits for them, and re-layouts  9.67 us (9%)
    pallas_call x1, Pallas kernels, per_device(): pl.pallas_call(kernel, out_shape=(jax.ShapeDtypeStruct(queries.shape, BF1...  96.5 us
    unnamed x17, local copies, waits for them, and re-layouts  9.67 us

profile of v1, /device:TPU:100, one launch (start us, length us, event | category | flops | bytes accessed | tf_op | source)
XLA Modules:
  0.0 106.8 jit_solution(11545613863901041720)
XLA Ops:
  0.6 0.8 copy.11.chosen_ref
  1.4 0.0 copy-start
  1.4 1.2 %copy-done = bf16[1,128,4096]{2,1,0:T(8,128)(2,1)S(1)} copy-done((bf16[1,128,4096]{2,1,0:T(8,128)(2,1)S(1)}, bf16[1,128,4096]{2,1,0:T(8,128)(2,1)}, u32[]{:S(2)}) %copy-start) | copy-done | bytes 1048600
  2.6 0.0 copy-start.1
  2.6 1.2 %copy-done.1 = bf16[1,128,4096]{2,1,0:T(8,128)(2,1)S(1)} copy-done((bf16[1,128,4096]{2,1,0:T(8,128)(2,1)S(1)}, bf16[1,128,4096]{2,1,0:T(8,128)(2,1)}, u32[]{:S(2)}) %copy-start.1) | copy-done | bytes 1048600
  3.8 0.0 copy-start.2
  3.8 0.9 copy-done.2
  4.8 0.0 copy-start.3
  4.8 0.9 copy-done.3
  5.7 0.0 copy-start.4
  5.7 0.7 copy-done.4
  6.4 0.0 copy-start.5
  6.4 0.7 copy-done.5
  7.1 96.5 %block_attention_backward.1 = (bf16[1,128,4096]{2,1,0:T(8,128)(2,1)S(1)}, bf16[1,128,512]{2,1,0:T(8,128)(2,1)S(1)}, bf16[1,128,512]{2,1,0:T(8,128)(2,1)S(1)}, bf16[1,128,4096]{2,1,0:T(8,128)(2,1)S(1)}) custom-call(s32[1,4,2]{2,1,0:T(4,128)S(1)} %copy.11.chosen_ref, bf16[1,128,4096]{2,1,0:T(8,128)(2,1)S(1)} %copy-done, bf16[1,128,512]{2,1,0:T(8,128)(2,1)S(1)} %copy-done.2, ...), custom_call_target="tpu_custom_call" | custom-call | flops 8053063680 | bytes 6291456 | tf_op jit(solution)/shard_map/block_attention_backward/pallas_call | solution.py:481
  103.6 1.0 copy.16
  104.5 0.7 copy.17
  105.2 0.7 copy.18
  105.9 1.0 copy.19
Async XLA Ops:
  1.4 1.2 %copy-start = (bf16[1,128,4096]{2,1,0:T(8,128)(2,1)S(1)}, bf16[1,128,4096]{2,1,0:T(8,128)(2,1)}, u32[]{:S(2)}) copy-start(bf16[1,128,4096]{2,1,0:T(8,128)(2,1)} %q_ref.1) | copy-start | bytes 3145732
  2.6 1.2 %copy-start.1 = (bf16[1,128,4096]{2,1,0:T(8,128)(2,1)S(1)}, bf16[1,128,4096]{2,1,0:T(8,128)(2,1)}, u32[]{:S(2)}) copy-start(bf16[1,128,4096]{2,1,0:T(8,128)(2,1)} %g_ref.1) | copy-start | bytes 3145732
  3.8 0.9 copy-start.2
  4.8 0.9 copy-start.3
  5.7 0.7 copy-start.4
  6.4 0.7 copy-start.5

commit v2 on v1

v2 whole, which is shorter than its diff:
```python
import jax
import jax.numpy as jnp
from jax import lax
from jax.experimental import pallas as pl
from jax.experimental.pallas import tpu as pltpu
from jax.sharding import PartitionSpec as P

H = 32
KVH = 4
HD = 128
BLOCK = 512
ROWS = 128
PAIR = 2 * ROWS
SLOTS = 6
LEVELS = 8
LOG2E = 1.4426950408889634
SCALE = HD**-0.5
HEADS = 4
NT = (((1,), (1,)), ((), ()))
NN = (((1,), (0,)), ((), ()))
TN = (((0,), (0,)), ((), ()))
MESH = pl.DeviceIdType.MESH
F32 = jnp.float32
BF16 = jnp.bfloat16


def kernel(
    chosen_ref, q_ref, k_ref, v_ref, g_ref, lse_ref, delta_ref,
    dq_ref, dk_ref, dv_ref, hb_ref,
    qa, ga, kv, wr, acc, dqt, stat, stat_in, rs, rr, rs_wide, rr_wide, es, er, dq_out, fin,
    own_sem, x_s, x_r, qx_s, qx_r, up_s, up_r, w_s, w_r, e_s, e_r,
    rd_s, rd_r, er_s, er_r, dq_s, dq_r, hb_s, hb_r, f_s, f_r,
):
    pipe = lax.axis_index("pipe")
    place = lax.axis_index("ctx")
    z = place // 2
    xh = place % 2
    xo = 1 - xh

    def level(number):
        return (pipe, number * 2 + xh)

    partner = (pipe, z * 2 + xo)
    above = level((z + 1) % LEVELS)
    below = level((z + LEVELS - 1) % LEVELS)
    before = ((pipe + 15) % 16, place)
    after = ((pipe + 1) % 16, place)
    chain = jnp.where(z <= 5, z, z - 4)
    chain_above = jnp.where(z <= 4, z + 1, jnp.where(z == 7, 0, z - 3))
    last_block = z >= 6
    second = (chosen_ref[0, 0, 3] + chosen_ref[0, 1, 3]) == 3

    def remote(src, dst, send, recv, device):
        return pltpu.make_async_remote_copy(
            src_ref=src, dst_ref=dst, send_sem=send, recv_sem=recv,
            device_id=device, device_id_type=MESH,
        )

    def lanes(start, size):
        return pl.ds(pl.multiple_of(start, 128), size)

    def rows(start, size):
        return pl.ds(pl.multiple_of(start, 128), size)

    def kv_swap(j, t):
        src = (k_ref, v_ref)[t]
        return remote(
            src.at[0, :, lanes((2 * xo + j) * HD, HD)],
            kv.at[j, 0, t, rows(xh * ROWS, ROWS)],
            x_s.at[j, t], x_r.at[j, t], partner,
        )

    def kv_own(j, t):
        src = (k_ref, v_ref)[t]
        return pltpu.make_async_copy(
            src.at[0, :, lanes((2 * xh + j) * HD, HD)],
            kv.at[j, 0, t, rows(xh * ROWS, ROWS)],
            own_sem.at[j, t],
        )

    def q_swap(j, t):
        src, dst = ((q_ref, qa), (g_ref, ga))[t]
        return remote(
            src.at[0, :, lanes(xo * 2048 + j * 1024, 1024)],
            dst.at[xh, :, pl.ds(j * 1024, 1024)],
            qx_s.at[j, t], qx_r.at[j, t], partner,
        )

    def q_own(j, t):
        src, dst = ((q_ref, qa), (g_ref, ga))[t]
        return pltpu.make_async_copy(
            src.at[0, :, lanes(xh * 2048 + j * 1024, 1024)],
            dst.at[xh, :, pl.ds(j * 1024, 1024)],
            own_sem.at[2 + j, t],
        )

    def stat_swap(t):
        src = (lse_ref, delta_ref)[t]
        return remote(
            src.at[0, pl.ds(pl.multiple_of(xo * 16, 16), 16)],
            stat_in.at[0, t], x_s.at[2, t], x_r.at[2, t], partner,
        )

    def stat_own(t):
        src = (lse_ref, delta_ref)[t]
        return pltpu.make_async_copy(
            src.at[0, pl.ds(pl.multiple_of(xh * 16, 16), 16)],
            stat_in.at[1, t], own_sem.at[4, t],
        )

    def up(j, d, t):
        return remote(
            kv.at[j, d, t], kv.at[j, d + 1, t], up_s.at[j, d, t], up_r.at[j, d + 1, t], above
        )

    def up_in(j, d, t):
        return remote(
            kv.at[j, d - 1, t], kv.at[j, d, t], up_s.at[j, d - 1, t], up_r.at[j, d, t], above
        )

    def round_first(j, t):
        return remote(
            kv.at[j, 0, t], wr.at[j, z, t], w_s.at[j, 0, t], w_r.at[j, z, t],
            level(jnp.where(z == 3, 1, 7)),
        )

    def round_on(j, t):
        return remote(
            wr.at[j, 3, t], wr.at[j, 3, t], w_s.at[j, 1, t], w_r.at[j, 3, t], level(7)
        )

    def round_in(j, source, t):
        return remote(
            wr.at[j, source, t], wr.at[j, source, t], w_s.at[j, 0, t], w_r.at[j, source, t],
            level(7),
        )

    def extra(j, e, t):
        return remote(
            kv.at[j, 4 + e, t], kv.at[j, 4 + e, t], e_s.at[j, e, t], e_r.at[j, e, t], below
        )

    def down(j, d, t):
        return remote(
            rs.at[j, d, t], rr.at[j, d - 1, t], rd_s.at[j, d, t], rd_r.at[j, d - 1, t], below
        )

    def down_wide(j, d, t):
        return remote(
            rs_wide.at[j, d - 1, t], rr_wide.at[j, d - 1, t],
            rd_s.at[j, d, t], rd_r.at[j, d - 1, t], below,
        )

    def down_in(j, d, t):
        return remote(
            rr.at[j, d, t], rr.at[j, d, t], rd_s.at[j, d + 1, t], rd_r.at[j, d, t], below
        )

    def down_wide_in(j, d, t):
        return remote(
            rr_wide.at[j, d, t], rr_wide.at[j, d, t],
            rd_s.at[j, d + 1, t], rd_r.at[j, d, t], below,
        )

    def extra_back(j, e, t, target, way):
        return remote(es.at[j, e, t], er.at[j, e, t], er_s.at[j, way, t], er_r.at[j, e, t], target)

    def extra_on(j, t):
        return remote(er.at[j, 1, t], er.at[j, 1, t], er_s.at[j, 1, t], er_r.at[j, 1, t], level(3))

    def extra_in(j, e, t):
        return remote(er.at[j, e, t], er.at[j, e, t], er_s.at[j, e, t], er_r.at[j, e, t], above)

    def dq_swap(j):
        return remote(
            dq_out.at[j], dq_ref.at[0, :, lanes(xh * 2048 + j * 1024, 1024)],
            dq_s.at[j], dq_r.at[j], partner,
        )

    def dq_in(j):
        return remote(
            dq_out.at[j], dq_ref.at[0, :, lanes(xo * 2048 + j * 1024, 1024)],
            dq_s.at[j], dq_r.at[j], partner,
        )

    def hand_back(j, column):
        part = lanes(column * 2048 + j * 1024, 1024)
        return remote(
            dq_ref.at[0, :, part], hb_ref.at[0, :, part],
            hb_s.at[j, column], hb_r.at[j, column], before,
        )

    def fin_swap(j, t):
        dst = (dk_ref, dv_ref)[t]
        return remote(
            fin.at[j, t, rows(xo * ROWS, ROWS)],
            dst.at[0, :, lanes((2 * xh + j) * HD, HD)],
            f_s.at[j, t], f_r.at[j, t], partner,
        )

    def unit(j, r, d, first, masked=False):
        keys = kv[j, d, 0]
        values = kv[j, d, 1]
        d_keys = None
        d_values = None
        for c in range(8 // HEADS):
            base = j * 1024 + c * HEADS * HD
            head = j * 8 + c * HEADS
            queries = jnp.concatenate(
                [qa[r, :, base + i * HD : base + (i + 1) * HD] for i in range(HEADS)], axis=0
            )
            grads = jnp.concatenate(
                [ga[r, :, base + i * HD : base + (i + 1) * HD] for i in range(HEADS)], axis=0
            )
            lse = jnp.concatenate(
                [stat[0, r, pl.ds(head + i, 1), :] for i in range(HEADS)], axis=1
            )
            delta = jnp.concatenate(
                [stat[1, r, pl.ds(head + i, 1), :] for i in range(HEADS)], axis=1
            )
            scores = lax.dot_general(keys, queries, NT, preferred_element_type=F32)
            probs = jnp.exp2(scores * (SCALE * LOG2E) - lse)
            if masked:
                shape = (PAIR, HEADS * HD)
                key_at = lax.broadcasted_iota(jnp.int32, shape, 0)
                query_at = lax.broadcasted_iota(jnp.int32, shape, 1) % HD + r * ROWS
                probs = jnp.where(key_at <= query_at, probs, 0.0)
            prob_grads = lax.dot_general(values, grads, NT, preferred_element_type=F32)
            score_grads = (probs * (prob_grads - delta)).astype(BF16)
            probs_low = probs.astype(BF16)
            part_v = lax.dot_general(probs_low, grads, NN, preferred_element_type=F32)
            part_k = lax.dot_general(score_grads, queries, NN, preferred_element_type=F32)
            d_values = part_v if d_values is None else d_values + part_v
            d_keys = part_k if d_keys is None else d_keys + part_k
            dqt[r, :, base : base + HEADS * HD] += lax.dot_general(
                keys, score_grads, TN, preferred_element_type=F32
            )
        if first:
            acc[j, d, 0] = d_keys
            acc[j, d, 1] = d_values
        else:
            acc[j, d, 0] += d_keys
            acc[j, d, 1] += d_values

    def has(d):
        return (d <= chain) | (last_block & (d >= 4))

    def arrival(t):
        low = jnp.where((t > z) & (t <= 2 * z), 2 * z + 1 - t, 0)
        five = jnp.where(t == 6, 1, jnp.where(t > 6, 12 - t, 0))
        six = jnp.where(t == 3, 1, jnp.where(t == 7, 2, 0))
        seven = jnp.where(t == 3, 1, jnp.where(t == 4, 2, jnp.where(t == 8, 3, 0)))
        return jnp.where(
            z <= 4, low, jnp.where(z == 5, five, jnp.where(z == 6, six, seven))
        )

    def take(j, d):
        for t in range(2):
            up_in(j, d, t).wait_recv()

            @pl.when(d + 1 <= chain_above)
            def _():
                up(j, d, t).start()

    def choose(j, e):
        kv[j, 4 + e] = jnp.where(second, wr[j, 2 + e], wr[j, e])
        for t in range(2):
            extra(j, e, t).start()

    def extra_levels(j, k):
        @pl.when((z == 1) & (k == 2))
        def _():
            for t in range(2):
                round_in(j, 3, t).wait_recv()
                round_on(j, t).start()

        for e in range(2):
            @pl.when((z == 7) & (k == 3 + e))
            def _():
                for t in range(2):
                    round_in(j, e, t).wait_recv()
                    round_in(j, 2 + e, t).wait_recv()
                choose(j, e)

            @pl.when((z == 6) & (k == 4 + e))
            def _():
                for t in range(2):
                    extra(j, e, t).wait_recv()

    def gather(t):
        @pl.when(t <= chain)
        def _():
            take(0, t)

        slot = arrival(t)

        @pl.when(slot >= 1)
        def _():
            take(1, slot)

        at = jnp.where(z <= 3, jnp.maximum(2 * z, 1), jnp.where(z == 4, 4, 2))

        @pl.when((t == at) & (chain_above >= 1))
        def _():
            for kind in range(2):
                up(1, 0, kind).start()

        @pl.when((t == 3) & (z <= 3))
        def _():
            for kind in range(2):
                round_first(1, kind).start()

        extra_levels(0, t)
        extra_levels(1, t - 4)

    def starts_chain(d):
        return d + 1 > chain_above

    def send_first(j, d):
        @pl.when((d <= chain) & starts_chain(d))
        def _():
            for t in range(2):
                rs[j, d, t] = acc[j, d, t].astype(BF16)
                down(j, d, t).start()

        @pl.when((z == 6) & (d >= 4))
        def _():
            for t in range(2):
                es[j, d - 4, t] = acc[j, d, t].astype(BF16)
                extra_back(j, d - 4, t, above, d - 4).start()

    def send_on(j, d):
        due = (d >= 1) & (d <= chain) & jnp.logical_not(starts_chain(d))

        @pl.when(due & (z >= 3))
        def _():
            for t in range(2):
                down_in(j, d, t).wait_recv()
                rs[j, d, t] = (acc[j, d, t] + rr[j, d, t].astype(F32)).astype(BF16)
                down(j, d, t).start()

        @pl.when(due & (z == 2))
        def _():
            for t in range(2):
                down_in(j, d, t).wait_recv()
                rs_wide[j, d - 1, t] = acc[j, d, t] + rr[j, d, t].astype(F32)
                down_wide(j, d, t).start()

        @pl.when(due & (z == 1))
        def _():
            for t in range(2):
                down_wide_in(j, d, t).wait_recv()
                rs_wide[j, d - 1, t] = acc[j, d, t] + rr_wide[j, d, t]
                down_wide(j, d, t).start()

    def extra_sum(j, e):
        @pl.when(z == 7)
        def _():
            for t in range(2):
                extra_in(j, e, t).wait_recv()
                es[j, e, t] = (acc[j, 4 + e, t] + er[j, e, t].astype(F32)).astype(BF16)
                if e == 0:
                    extra_back(j, 0, t, level(0), 0).start()
                    extra_back(j, 0, t, level(2), 2).start()
                else:
                    extra_back(j, 1, t, level(1), 1).start()

    def extra_relay(j):
        @pl.when(z == 1)
        def _():
            for t in range(2):
                extra_in(j, 1, t).wait_recv()
                extra_on(j, t).start()

    def finish_keys(j):
        @pl.when(z <= 3)
        def _():
            e = z % 2

            @pl.when(z != 1)
            def _():
                for t in range(2):
                    extra_in(j, e, t).wait_recv()

            mine = second == (z >= 2)
            acc[j, 0] += jnp.where(mine, er[j, e].astype(F32), 0.0)

        for t in range(2):
            @pl.when((z >= 2) & (z <= 6))
            def _():
                down_in(j, 0, t).wait_recv()
                acc[j, 0, t] += rr[j, 0, t].astype(F32)

            @pl.when(z <= 1)
            def _():
                down_wide_in(j, 0, t).wait_recv()
                acc[j, 0, t] += rr_wide[j, 0, t]

            fin[j, t] = (acc[j, 0, t] * (SCALE if t == 0 else 1.0)).astype(BF16)
            fin_swap(j, t).start()
        columns = lanes((2 * xh + j) * HD, HD)
        dk_ref[0, :, columns] = fin[j, 0, rows(xh * ROWS, ROWS)]
        dv_ref[0, :, columns] = fin[j, 1, rows(xh * ROWS, ROWS)]

    def finish_queries(j):
        for i in range(8):
            cols = slice(j * 1024 + i * HD, j * 1024 + (i + 1) * HD)
            dq_out[j, :, i * HD : (i + 1) * HD] = (dqt[xo, :, cols].T * SCALE).astype(BF16)
        dq_swap(j).start()
        for i in range(8):
            cols = slice(j * 1024 + i * HD, j * 1024 + (i + 1) * HD)
            dq_ref[0, :, lanes(xh * 2048 + j * 1024 + i * HD, HD)] = (
                dqt[xh, :, cols].T * SCALE
            ).astype(BF16)

        @pl.when(pipe > 0)
        def _():
            hand_back(j, xh).start()

    def hand_on(j):
        dq_in(j).wait_recv()

        @pl.when(pipe > 0)
        def _():
            hand_back(j, xo).start()

    for j in range(2):
        for t in range(2):
            kv_own(j, t).start()
    for t in range(2):
        stat_own(t).start()
        for j in range(2):
            q_own(j, t).start()

    barrier = pltpu.get_barrier_semaphore()

    def greet(device):
        pl.semaphore_signal(barrier, inc=1, device_id=device, device_id_type=MESH)

    for device in (partner, above, below, before, after):
        greet(device)

    @pl.when((z == 1) | (z == 2))
    def _():
        greet(level(7))

    @pl.when(z == 7)
    def _():
        greet(level(1))
        greet(level(2))

    @pl.when(z == 1)
    def _():
        greet(level(3))

    @pl.when(z == 3)
    def _():
        greet(level(1))

    far_greetings = jnp.where((z == 1) | (z == 7), 2, jnp.where((z == 2) | (z == 3), 1, 0))
    pl.semaphore_wait(barrier, 5 + far_greetings)

    for j in range(2):
        for t in range(2):
            kv_swap(j, t).start()
        if j == 0:
            for t in range(2):
                stat_swap(t).start()

    dqt[...] = jnp.zeros_like(dqt)

    @pl.when(pipe == 15)
    def _():
        hb_ref[...] = jnp.zeros_like(hb_ref)

    for t in range(2):
        stat_own(t).wait()
    stat[0, xh] = stat_in[1, 0].astype(F32) * LOG2E
    stat[1, xh] = stat_in[1, 1].astype(F32)
    for j in range(2):
        for t in range(2):
            kv_own(j, t).wait()
            q_own(j, t).wait()

    for t in range(2):
        kv_swap(0, t).wait_recv()

        @pl.when(chain_above >= 1)
        def _():
            up(0, 0, t).start()

        @pl.when(z <= 3)
        def _():
            round_first(0, t).start()

    for j in range(2):
        for t in range(2):
            q_swap(j, t).start()
    for t in range(2):
        kv_swap(1, t).wait_recv()
        stat_swap(t).wait_recv()
    stat[0, xo] = stat_in[0, 0].astype(F32) * LOG2E
    stat[1, xo] = stat_in[0, 1].astype(F32)

    unit(0, xh, 0, True, True)

    def phase_a(k, carry):
        gather(k)

        @pl.when(has(k))
        def _():
            unit(0, xh, k, True)

        return carry

    lax.fori_loop(1, SLOTS, phase_a, 0)
    for t in range(2):
        q_swap(0, t).wait_recv()

    def arrived(k):
        return jnp.where(
            last_block, k, jnp.where(z == 5, jnp.where(k == 1, 1, 7 - k), chain + 1 - k)
        )

    def own_rows(k):
        d = arrived(k)

        @pl.when((d >= 1) & has(d))
        def _():
            unit(1, xh, d, True)

    def partner_rows(j, d):
        @pl.when((d >= 1) & has(d))
        def _():
            unit(j, xo, d, False)
            send_first(j, d)

    unit(1, xh, 0, True, True)

    def phase_b(k, carry):
        gather(k + 5)

        def one(n, inner):
            partner_rows(0, 7 - 2 * k - n)
            return inner

        lax.fori_loop(0, 2, one, 0)
        own_rows(k)
        return carry

    lax.fori_loop(1, 3, phase_b, 0)
    gather(8)
    partner_rows(0, 1)
    unit(0, xo, 0, False, True)
    finish_queries(0)
    own_rows(3)
    for e in (1, 0):
        extra_sum(0, e)
    send_on(0, 4)
    for t in range(2):
        q_swap(1, t).wait_recv()

    def phase_c(k, carry):
        gather(k + 5)
        own_rows(k)
        partner_rows(1, arrived(k - 2))
        send_on(0, 7 - k)
        return carry

    lax.fori_loop(4, 6, phase_c, 0)
    hand_on(0)

    def phase_d(n, carry):
        partner_rows(1, arrived(jnp.where(n == 2, 1, 4 + n)))

        @pl.when(n == 0)
        def _():
            send_on(0, 1)

        return carry

    lax.fori_loop(0, 3, phase_d, 0)
    extra_relay(0)
    unit(1, xo, 0, False, True)
    finish_queries(1)
    for e in range(2):
        extra_sum(1, e)

    def phase_e(k, carry):
        send_on(1, SLOTS - k)
        return carry

    extra_relay(1)
    lax.fori_loop(1, 3, phase_e, 0)
    finish_keys(0)
    hand_on(1)
    lax.fori_loop(3, SLOTS, phase_e, 0)
    finish_keys(1)

    for j in range(2):
        for t in range(2):
            fin_swap(j, t).wait_recv()
            fin_swap(j, t).wait_send()
            kv_swap(j, t).wait_send()
            q_swap(j, t).wait_send()
        dq_swap(j).wait_send()

        @pl.when(pipe > 0)
        def _():
            for column in range(2):
                hand_back(j, column).wait_send()

        @pl.when(pipe < 15)
        def _():
            for column in range(2):
                hand_back(j, column).wait_recv()

        for t in range(2):
            for d in range(SLOTS):
                @pl.when(d + 1 <= chain_above)
                def _():
                    up(j, d, t).wait_send()

                if d >= 1:
                    @pl.when((d <= chain) & (z >= 3))
                    def _():
                        down(j, d, t).wait_send()

                if d == 1 or d == 2:
                    @pl.when((d <= chain) & (z <= 2))
                    def _():
                        down_wide(j, d, t).wait_send()

            @pl.when(z <= 3)
            def _():
                round_first(j, t).wait_send()

            @pl.when(z == 1)
            def _():
                round_on(j, t).wait_send()
                extra_on(j, t).wait_send()

            for e in range(2):
                @pl.when(z == 7)
                def _():
                    extra(j, e, t).wait_send()

                @pl.when(last_block)
                def _():
                    extra_back(j, e, t, above, e).wait_send()

            @pl.when(z == 7)
            def _():
                extra_back(j, 0, t, level(2), 2).wait_send()

    for t in range(2):
        stat_swap(t).wait_send()


def write_out(*refs):
    done = refs[12]

    def piece(stage, i, c):
        part = pl.ds(c * 32, 32)
        return pltpu.make_async_copy(
            refs[(i, 8 + i)[stage]].at[0, part], refs[(8 + i, 4 + i)[stage]].at[0, part],
            done.at[stage, i, c],
        )

    pieces = [(i, c) for i in (0, 3, 1, 2) for c in range(4)]
    for i, c in pieces:
        piece(0, i, c).start()
    for i, c in pieces:
        piece(0, i, c).wait()
        piece(1, i, c).start()
    for i, c in pieces:
        piece(1, i, c).wait()


def per_device(queries, key_heads, value_heads, out_grad, log_sum, row_delta, chosen):
    vmem = pl.BlockSpec(memory_space=pltpu.VMEM)
    hbm = pl.BlockSpec(memory_space=pltpu.HBM)
    dma = pltpu.SemaphoreType.DMA
    level = (2, PAIR, HD)
    flops = 5 * 2 * ROWS * H * HD * 1536
    grads = pl.pallas_call(
        kernel,
        out_shape=(
            jax.ShapeDtypeStruct(queries.shape, BF16),
            jax.ShapeDtypeStruct(key_heads.shape, BF16),
            jax.ShapeDtypeStruct(value_heads.shape, BF16),
            jax.ShapeDtypeStruct(queries.shape, BF16),
        ),
        in_specs=[pl.BlockSpec(memory_space=pltpu.SMEM)] + [hbm] * 6,
        out_specs=(vmem,) * 4,
        scratch_shapes=[
            pltpu.VMEM((2, ROWS, 2048), BF16),
            pltpu.VMEM((2, ROWS, 2048), BF16),
            pltpu.VMEM((2, SLOTS) + level, BF16),
            pltpu.VMEM((2, 4) + level, BF16),
            pltpu.VMEM((2, SLOTS) + level, F32),
            pltpu.VMEM((2, HD, 2048), F32),
            pltpu.VMEM((2, 2, 16, ROWS), F32),
            pltpu.VMEM((2, 2, 16, ROWS), BF16),
            pltpu.VMEM((2, SLOTS) + level, BF16),
            pltpu.VMEM((2, SLOTS) + level, BF16),
            pltpu.VMEM((2, 2) + level, F32),
            pltpu.VMEM((2, 2) + level, F32),
            pltpu.VMEM((2, 2) + level, BF16),
            pltpu.VMEM((2, 2) + level, BF16),
            pltpu.VMEM((2, ROWS, 1024), BF16),
            pltpu.VMEM((2,) + level, BF16),
            dma((5, 2)),
            dma((3, 2)), dma((3, 2)),
            dma((2, 2)), dma((2, 2)),
            dma((2, SLOTS, 2)), dma((2, SLOTS, 2)),
            dma((2, 2, 2)), dma((2, 4, 2)),
            dma((2, 2, 2)), dma((2, 2, 2)),
            dma((2, SLOTS, 2)), dma((2, SLOTS, 2)),
            dma((2, 3, 2)), dma((2, 2, 2)),
            dma((2,)), dma((2,)),
            dma((2, 2)), dma((2, 2)),
            dma((2, 2)), dma((2, 2)),
        ],
        compiler_params=pltpu.CompilerParams(
            collective_id=0, has_side_effects=True, vmem_limit_bytes=63 * 2**20
        ),
        cost_estimate=pl.CostEstimate(
            flops=flops, bytes_accessed=6 * 2**20, transcendentals=ROWS * H * 1536
        ),
        name="block_attention_backward",
    )(chosen.transpose(0, 2, 1), queries, key_heads, value_heads, out_grad, log_sum, row_delta)
    anywhere = pl.BlockSpec(memory_space=pl.ANY)
    return pl.pallas_call(
        write_out,
        out_shape=tuple(jax.ShapeDtypeStruct(part.shape, part.dtype) for part in grads),
        in_specs=[anywhere] * 4,
        out_specs=(anywhere,) * 4,
        scratch_shapes=[pltpu.VMEM(part.shape, part.dtype) for part in grads] + [dma((2, 4, 4))],
        name="write_out",
    )(*grads)


def solution(mesh):
    heads = P("pipe", "ctx", None)
    stats = P("pipe", None, "ctx")
    return jax.shard_map(
        per_device,
        mesh=mesh,
        in_specs=(heads, heads, heads, heads, stats, stats, P("pipe", None, None)),
        out_specs=(heads, heads, heads, heads),
        check_vma=False,
    )
```

time: 107 us -> 89.5 us (0.84)
  the two profiles are of different devices: /device:TPU:100 before, /device:TPU:8 now
where the time goes in v2:
time: 89.5 us; the launch traced here: 88.7 us
  Pallas kernels  87.9 us (98%)
    pallas_call x1, Pallas kernels, per_device(): pl.pallas_call(kernel, out_shape=(jax.ShapeDtypeStruct(queries.shape, BF1...  85.3 us
    pallas_call x1, Pallas kernels, per_device(): pl.pallas_call(write_out, out_shape=tuple((jax.ShapeDtypeStruct(part.shap...  2.61 us

profile of v2, /device:TPU:8, one launch (start us, length us, event | category | flops | bytes accessed | tf_op | source)
XLA Modules:
  0.0 88.7 jit_solution(3037065834671235790)
XLA Ops:
  0.6 85.3 %block_attention_backward.1 = (bf16[1,128,4096]{2,1,0:T(8,128)(2,1)}, bf16[1,128,512]{2,1,0:T(8,128)(2,1)}, bf16[1,128,512]{2,1,0:T(8,128)(2,1)}, bf16[1,128,4096]{2,1,0:T(8,128)(2,1)}) custom-call(s32[1,2,4]{2,1,0:T(2,128)} %bitcast.1, bf16[1,128,4096]{2,1,0:T(8,128)(2,1)} %q_ref.1, bf16[1,128,512]{2,1,0:T(8,128)(2,1)} %k_ref.1, ...), custom_call_target="tpu_custom_call" | custom-call | flops 8053063680 | bytes 6291456 | tf_op jit(solution)/shard_map/block_attention_backward/pallas_call | solution.py:686
  85.9 2.6 %write_out.1 = (bf16[1,128,4096]{2,1,0:T(8,128)(2,1)}, bf16[1,128,512]{2,1,0:T(8,128)(2,1)}, bf16[1,128,512]{2,1,0:T(8,128)(2,1)}, bf16[1,128,4096]{2,1,0:T(8,128)(2,1)}) custom-call(bf16[1,128,4096]{2,1,0:T(8,128)(2,1)} %get-tuple-element.8.refs_0_, bf16[1,128,512]{2,1,0:T(8,128)(2,1)} %get-tuple-element.9.refs_1_, ...), custom_call_target="tpu_custom_call" | custom-call | tf_op jit(solution)/shard_map/write_out/pallas_call | solution.py:734

commit v3 on v2

--- a/solution.py
+++ b/solution.py
@@ -15,7 +15,7 @@
 LEVELS = 8
 LOG2E = 1.4426950408889634
 SCALE = HD**-0.5
-HEADS = 4
+HEADS = 8
 NT = (((1,), (1,)), ((), ()))
 NN = (((1,), (0,)), ((), ()))
 TN = (((0,), (0,)), ((), ()))
@@ -359,11 +359,10 @@
             for t in range(2):
                 extra_in(j, e, t).wait_recv()
                 es[j, e, t] = (acc[j, 4 + e, t] + er[j, e, t].astype(F32)).astype(BF16)
-                if e == 0:
-                    extra_back(j, 0, t, level(0), 0).start()
+                extra_back(j, e, t, level(e), e).start()
+            if e == 1:
+                for t in range(2):
                     extra_back(j, 0, t, level(2), 2).start()
-                else:
-                    extra_back(j, 1, t, level(1), 1).start()
 
     def extra_relay(j):
         @pl.when(z == 1)
@@ -513,7 +512,8 @@
 
         return carry
 
-    lax.fori_loop(1, SLOTS, phase_a, 0)
+    unit(1, xh, 0, True, True)
+    lax.fori_loop(1, 4, phase_a, 0)
     for t in range(2):
         q_swap(0, t).wait_recv()
 
@@ -535,28 +535,25 @@
             unit(j, xo, d, False)
             send_first(j, d)
 
-    unit(1, xh, 0, True, True)
-
     def phase_b(k, carry):
-        gather(k + 5)
-
-        def one(n, inner):
-            partner_rows(0, 7 - 2 * k - n)
-            return inner
-
-        lax.fori_loop(0, 2, one, 0)
-        own_rows(k)
+        phase_a(k, carry)
+        partner_rows(0, k - 3)
         return carry
 
-    lax.fori_loop(1, 3, phase_b, 0)
-    gather(8)
-    partner_rows(0, 1)
+    lax.fori_loop(4, SLOTS, phase_b, 0)
+    gather(6)
+
+    def first_far(n, carry):
+        partner_rows(0, 5 - n)
+        return carry
+
+    lax.fori_loop(0, 2, first_far, 0)
+    own_rows(1)
+    gather(7)
+    partner_rows(0, 3)
     unit(0, xo, 0, False, True)
     finish_queries(0)
-    own_rows(3)
-    for e in (1, 0):
-        extra_sum(0, e)
-    send_on(0, 4)
+    own_rows(2)
     for t in range(2):
         q_swap(1, t).wait_recv()
 
@@ -564,22 +561,28 @@
         gather(k + 5)
         own_rows(k)
         partner_rows(1, arrived(k - 2))
+        for e in range(2):
+            @pl.when(k == 3)
+            def _():
+                extra_sum(0, e)
+
         send_on(0, 7 - k)
         return carry
 
-    lax.fori_loop(4, 6, phase_c, 0)
+    lax.fori_loop(3, 6, phase_c, 0)
     hand_on(0)
 
     def phase_d(n, carry):
-        partner_rows(1, arrived(jnp.where(n == 2, 1, 4 + n)))
+        partner_rows(1, arrived(4 + n))
 
         @pl.when(n == 0)
         def _():
             send_on(0, 1)
+            send_on(1, 4)
 
         return carry
 
-    lax.fori_loop(0, 3, phase_d, 0)
+    lax.fori_loop(0, 2, phase_d, 0)
     extra_relay(0)
     unit(1, xo, 0, False, True)
     finish_queries(1)
@@ -590,11 +593,11 @@
         send_on(1, SLOTS - k)
         return carry
 
-    extra_relay(1)
-    lax.fori_loop(1, 3, phase_e, 0)
+    lax.fori_loop(3, 4, phase_e, 0)
     finish_keys(0)
     hand_on(1)
-    lax.fori_loop(3, SLOTS, phase_e, 0)
+    lax.fori_loop(4, SLOTS, phase_e, 0)
+    extra_relay(1)
     finish_keys(1)
 
     for j in range(2):

time: 89.5 us -> 84.5 us (0.944)
  Pallas kernels: 87.9 us -> 82.5 us
    pallas_call x1, Pallas kernels: 85.3 us -> 79.9 us  [per_device(): pl.pallas_call(kernel, out_shape=(jax.ShapeDtypeStruct(queries.shape, BF1...]
where the time goes in v3:
time: 84.5 us; the launch traced here: 83.3 us
  Pallas kernels  82.5 us (98%)
    pallas_call x1, Pallas kernels, per_device(): pl.pallas_call(kernel, out_shape=(jax.ShapeDtypeStruct(queries.shape, BF1...  79.9 us
    pallas_call x1, Pallas kernels, per_device(): pl.pallas_call(write_out, out_shape=tuple((jax.ShapeDtypeStruct(part.shap...  2.61 us

profile of v3, /device:TPU:8, one launch (start us, length us, event | category | flops | bytes accessed | tf_op | source)
XLA Modules:
  0.0 83.3 jit_solution(5516488794316261643)
XLA Ops:
  0.6 79.9 %block_attention_backward.1 = (bf16[1,128,4096]{2,1,0:T(8,128)(2,1)}, bf16[1,128,512]{2,1,0:T(8,128)(2,1)}, bf16[1,128,512]{2,1,0:T(8,128)(2,1)}, bf16[1,128,4096]{2,1,0:T(8,128)(2,1)}) custom-call(s32[1,2,4]{2,1,0:T(2,128)} %bitcast.1, bf16[1,128,4096]{2,1,0:T(8,128)(2,1)} %q_ref.1, bf16[1,128,512]{2,1,0:T(8,128)(2,1)} %k_ref.1, ...), custom_call_target="tpu_custom_call" | custom-call | flops 8053063680 | bytes 6291456 | tf_op jit(solution)/shard_map/block_attention_backward/pallas_call | solution.py:689
  80.5 2.6 %write_out.1 = (bf16[1,128,4096]{2,1,0:T(8,128)(2,1)}, bf16[1,128,512]{2,1,0:T(8,128)(2,1)}, bf16[1,128,512]{2,1,0:T(8,128)(2,1)}, bf16[1,128,4096]{2,1,0:T(8,128)(2,1)}) custom-call(bf16[1,128,4096]{2,1,0:T(8,128)(2,1)} %get-tuple-element.8.refs_0_, bf16[1,128,512]{2,1,0:T(8,128)(2,1)} %get-tuple-element.9.refs_1_, ...), custom_call_target="tpu_custom_call" | custom-call | tf_op jit(solution)/shard_map/write_out/pallas_call | solution.py:737

commit v4 on v3

--- a/solution.py
+++ b/solution.py
@@ -28,7 +28,7 @@
     chosen_ref, q_ref, k_ref, v_ref, g_ref, lse_ref, delta_ref,
     dq_ref, dk_ref, dv_ref, hb_ref,
     qa, ga, kv, wr, acc, dqt, stat, stat_in, rs, rr, rs_wide, rr_wide, es, er, dq_out, fin,
-    own_sem, x_s, x_r, qx_s, qx_r, up_s, up_r, w_s, w_r, e_s, e_r,
+    own_sem, x_s, x_r, qx_s, qx_r, first_s, up_s, up_r, w_s, w_r, e_s, e_r,
     rd_s, rd_r, er_s, er_r, dq_s, dq_r, hb_s, hb_r, f_s, f_r,
 ):
     pipe = lax.axis_index("pipe")
@@ -43,6 +43,8 @@
     partner = (pipe, z * 2 + xo)
     above = level((z + 1) % LEVELS)
     below = level((z + LEVELS - 1) % LEVELS)
+    across_above = (pipe, ((z + 1) % LEVELS) * 2 + xo)
+    across_below = (pipe, ((z + LEVELS - 1) % LEVELS) * 2 + xo)
     before = ((pipe + 15) % 16, place)
     after = ((pipe + 1) % 16, place)
     chain = jnp.where(z <= 5, z, z - 4)
@@ -111,6 +113,15 @@
     def up(j, d, t):
         return remote(
             kv.at[j, d, t], kv.at[j, d + 1, t], up_s.at[j, d, t], up_r.at[j, d + 1, t], above
+        )
+
+    def first_up(t, column):
+        src = (k_ref, v_ref)[t]
+        heads = (xh, xo)[column]
+        return remote(
+            src.at[0, :, lanes(2 * heads * HD, HD)],
+            kv.at[0, 1, t, rows(xh * ROWS, ROWS)],
+            first_s.at[column, t], up_r.at[0, 1, t], (above, across_above)[column],
         )
 
     def up_in(j, d, t):
@@ -436,7 +447,7 @@
     def greet(device):
         pl.semaphore_signal(barrier, inc=1, device_id=device, device_id_type=MESH)
 
-    for device in (partner, above, below, before, after):
+    for device in (partner, above, below, across_above, across_below, before, after):
         greet(device)
 
     @pl.when((z == 1) | (z == 2))
@@ -457,11 +468,17 @@
         greet(level(1))
 
     far_greetings = jnp.where((z == 1) | (z == 7), 2, jnp.where((z == 2) | (z == 3), 1, 0))
-    pl.semaphore_wait(barrier, 5 + far_greetings)
+    pl.semaphore_wait(barrier, 7 + far_greetings)
 
     for j in range(2):
         for t in range(2):
             kv_swap(j, t).start()
+            if j == 0:
+                @pl.when(chain_above >= 1)
+                def _():
+                    for column in (1, 0):
+                        first_up(t, column).start()
+
         if j == 0:
             for t in range(2):
                 stat_swap(t).start()
@@ -483,10 +500,6 @@
 
     for t in range(2):
         kv_swap(0, t).wait_recv()
-
-        @pl.when(chain_above >= 1)
-        def _():
-            up(0, 0, t).start()
 
         @pl.when(z <= 3)
         def _():
@@ -593,10 +606,10 @@
         send_on(1, SLOTS - k)
         return carry
 
-    lax.fori_loop(3, 4, phase_e, 0)
+    lax.fori_loop(3, 5, phase_e, 0)
     finish_keys(0)
     hand_on(1)
-    lax.fori_loop(4, SLOTS, phase_e, 0)
+    lax.fori_loop(5, SLOTS, phase_e, 0)
     extra_relay(1)
     finish_keys(1)
 
@@ -622,7 +635,11 @@
             for d in range(SLOTS):
                 @pl.when(d + 1 <= chain_above)
                 def _():
-                    up(j, d, t).wait_send()
+                    if j == 0 and d == 0:
+                        for column in range(2):
+                            first_up(t, column).wait_send()
+                    else:
+                        up(j, d, t).wait_send()
 
                 if d >= 1:
                     @pl.when((d <= chain) & (z >= 3))
@@ -716,6 +733,7 @@
             dma((5, 2)),
             dma((3, 2)), dma((3, 2)),
             dma((2, 2)), dma((2, 2)),
+            dma((2, 2)),
             dma((2, SLOTS, 2)), dma((2, SLOTS, 2)),
             dma((2, 2, 2)), dma((2, 4, 2)),
             dma((2, 2, 2)), dma((2, 2, 2)),

time: 84.5 us -> 83.7 us (level); the launches traced: 83.3 us -> 83.6 us
  no operation moved by 1% of the time
where the time goes in v4:
time: 83.7 us; the launch traced here: 83.6 us
  Pallas kernels  82.8 us (99%)
    pallas_call x1, Pallas kernels, per_device(): pl.pallas_call(kernel, out_shape=(jax.ShapeDtypeStruct(queries.shape, BF1...  80.2 us
    pallas_call x1, Pallas kernels, per_device(): pl.pallas_call(write_out, out_shape=tuple((jax.ShapeDtypeStruct(part.shap...  2.61 us

profile of v4, /device:TPU:8, one launch (start us, length us, event | category | flops | bytes accessed | tf_op | source)
XLA Modules:
  0.0 83.6 jit_solution(1147404346798190364)
XLA Ops:
  0.6 80.2 %block_attention_backward.1 = (bf16[1,128,4096]{2,1,0:T(8,128)(2,1)}, bf16[1,128,512]{2,1,0:T(8,128)(2,1)}, bf16[1,128,512]{2,1,0:T(8,128)(2,1)}, bf16[1,128,4096]{2,1,0:T(8,128)(2,1)}) custom-call(s32[1,2,4]{2,1,0:T(2,128)} %bitcast.1, bf16[1,128,4096]{2,1,0:T(8,128)(2,1)} %q_ref.1, bf16[1,128,512]{2,1,0:T(8,128)(2,1)} %k_ref.1, ...), custom_call_target="tpu_custom_call" | custom-call | flops 8053063680 | bytes 6291456 | tf_op jit(solution)/shard_map/block_attention_backward/pallas_call | solution.py:706
  80.8 2.6 %write_out.1 = (bf16[1,128,4096]{2,1,0:T(8,128)(2,1)}, bf16[1,128,512]{2,1,0:T(8,128)(2,1)}, bf16[1,128,512]{2,1,0:T(8,128)(2,1)}, bf16[1,128,4096]{2,1,0:T(8,128)(2,1)}) custom-call(bf16[1,128,4096]{2,1,0:T(8,128)(2,1)} %get-tuple-element.8.refs_0_, bf16[1,128,512]{2,1,0:T(8,128)(2,1)} %get-tuple-element.9.refs_1_, ...), custom_call_target="tpu_custom_call" | custom-call | tf_op jit(solution)/shard_map/write_out/pallas_call | solution.py:755

commit v5 on v4

--- a/solution.py
+++ b/solution.py
@@ -681,13 +681,13 @@
     done = refs[12]
 
     def piece(stage, i, c):
-        part = pl.ds(c * 32, 32)
+        part = pl.ds(c * 64, 64)
         return pltpu.make_async_copy(
             refs[(i, 8 + i)[stage]].at[0, part], refs[(8 + i, 4 + i)[stage]].at[0, part],
             done.at[stage, i, c],
         )
 
-    pieces = [(i, c) for i in (0, 3, 1, 2) for c in range(4)]
+    pieces = [(i, c) for i in (0, 3, 1, 2) for c in range(2)]
     for i, c in pieces:
         piece(0, i, c).start()
     for i, c in pieces:
@@ -757,7 +757,7 @@
         out_shape=tuple(jax.ShapeDtypeStruct(part.shape, part.dtype) for part in grads),
         in_specs=[anywhere] * 4,
         out_specs=(anywhere,) * 4,
-        scratch_shapes=[pltpu.VMEM(part.shape, part.dtype) for part in grads] + [dma((2, 4, 4))],
+        scratch_shapes=[pltpu.VMEM(part.shape, part.dtype) for part in grads] + [dma((2, 4, 2))],
         name="write_out",
     )(*grads)
 

time: 83.7 us -> 83.7 us (level)
  no operation moved by 1% of the time
where the time goes in v5:
time: 83.7 us; the launch traced here: 83.5 us
  Pallas kernels  82.7 us (99%)
    pallas_call x1, Pallas kernels, per_device(): pl.pallas_call(kernel, out_shape=(jax.ShapeDtypeStruct(queries.shape, BF1...  80.2 us
    pallas_call x1, Pallas kernels, per_device(): pl.pallas_call(write_out, out_shape=tuple((jax.ShapeDtypeStruct(part.shap...  2.57 us

profile of v5, /device:TPU:8, one launch (start us, length us, event | category | flops | bytes accessed | tf_op | source)
XLA Modules:
  0.0 83.5 jit_solution(11403458913194988919)
XLA Ops:
  0.6 80.2 %block_attention_backward.1 = (bf16[1,128,4096]{2,1,0:T(8,128)(2,1)}, bf16[1,128,512]{2,1,0:T(8,128)(2,1)}, bf16[1,128,512]{2,1,0:T(8,128)(2,1)}, bf16[1,128,4096]{2,1,0:T(8,128)(2,1)}) custom-call(s32[1,2,4]{2,1,0:T(2,128)} %bitcast.1, bf16[1,128,4096]{2,1,0:T(8,128)(2,1)} %q_ref.1, bf16[1,128,512]{2,1,0:T(8,128)(2,1)} %k_ref.1, ...), custom_call_target="tpu_custom_call" | custom-call | flops 8053063680 | bytes 6291456 | tf_op jit(solution)/shard_map/block_attention_backward/pallas_call | solution.py:706
  80.8 2.6 %write_out.1 = (bf16[1,128,4096]{2,1,0:T(8,128)(2,1)}, bf16[1,128,512]{2,1,0:T(8,128)(2,1)}, bf16[1,128,512]{2,1,0:T(8,128)(2,1)}, bf16[1,128,4096]{2,1,0:T(8,128)(2,1)}) custom-call(bf16[1,128,4096]{2,1,0:T(8,128)(2,1)} %get-tuple-element.8.refs_0_, bf16[1,128,512]{2,1,0:T(8,128)(2,1)} %get-tuple-element.9.refs_1_, ...), custom_call_target="tpu_custom_call" | custom-call | tf_op jit(solution)/shard_map/write_out/pallas_call | solution.py:755
